TPU v7x, 32 devices: a whole 2x2x4 slice. The times are simulated.
32 devices in a mesh: row: 8 (over z, y), col: 4 (over x, core).
Axes of the slice: x: 2, y: 2, z: 4, core: 2. Of those that a mesh axis runs over, the one named last changes fastest.
Arguments:
- activations: float32 [512, 12288], P('col', 'row'), may hold values from -1.5 to 1.5
- weights: float32 [12288, 24576], P('row', 'col'), may hold values from -0.21875 to 0.21875
- upstream: float32 [512, 24576], P('row', 'col'), may hold values from -6 to 6
Outputs:
- input_grad: float32 [512, 12288], P('col', 'row')
- weight_grad: float32 [12288, 24576], P('row', 'col')
All inputs are finite; a program needn't handle non-finite values.
Results may differ from a plain program's by a relative error of at most 0.00009.
Values sent between devices are 32-bit elements; how exact they have to be, the bound alone decides.
A program may use at most 192 MiB of HBM per device.

v0:
```python
import jax
import jax.numpy as jnp
from jax import lax
from jax.sharding import PartitionSpec as P

slope_scale = 0.7978845608028654
cubic_term = 0.044715


def gelu_slope(preact):
    inner = slope_scale * (preact + cubic_term * preact * preact * preact)
    tangent = jnp.tanh(inner)
    return 0.5 * (1.0 + tangent) + 0.5 * preact * (1.0 - tangent * tangent) * slope_scale * (
        1.0 + 3.0 * cubic_term * preact * preact
    )


def body(activations, weights, upstream):
    gathered = lax.all_gather(activations, "col", axis=0, tiled=True)
    partial_pre = jnp.dot(
        gathered, weights, precision=lax.Precision.HIGHEST, preferred_element_type=jnp.float32
    )
    shares = lax.psum_scatter(partial_pre, "row", scatter_dimension=0, tiled=True)
    delta_pre = lax.all_gather(upstream * gelu_slope(shares), "row", axis=0, tiled=True)
    weight_grad = lax.dot_general(
        gathered,
        delta_pre,
        (((0,), (0,)), ((), ())),
        precision=lax.Precision.HIGHEST,
        preferred_element_type=jnp.float32,
    )
    input_grad = lax.psum_scatter(
        lax.dot_general(
            delta_pre,
            weights,
            (((1,), (1,)), ((), ())),
            precision=lax.Precision.HIGHEST,
            preferred_element_type=jnp.float32,
        ),
        "col",
        scatter_dimension=0,
        tiled=True,
    )
    return (input_grad, weight_grad)


def solution(mesh):
    placed = (P("col", "row"), P("row", "col"), P("row", "col"))
    return jax.shard_map(
        body,
        mesh=mesh,
        in_specs=placed,
        out_specs=(P("col", "row"), P("row", "col")),
        check_vma=False,
    )
```

profile of v0, /device:TPU:0, one launch (start us, length us, event | category | flops | bytes accessed | tf_op | source)
XLA Modules:
  0.0 670.1 jit_solution(3940310768208907909)
XLA Ops:
  7.2 0.0 all-gather.3.cloned.1.call-start
  7.2 0.7 all-gather.3.cloned.1.call-update
  7.9 0.0 reduce-scatter.3.cloned.1.call-start
  7.9 32.9 %all-gather.3.cloned.1.call-done = f32[512,1536]{1,0:T(8,128)} async-done(((f32[128,1536]{1,0:T(8,128)}), f32[512,1536]{1,0:T(8,128)}) %all-gather.3.cloned.1.call-update) | async-done | bytes 3145744 | tf_op jit(solution)/shard_map/all_gather | solution.py:19
  40.8 66.6 %fusion.6 = f32[512,6144]{1,0:T(8,128)} fusion(f32[512,1536]{1,0:T(8,128)} %all-gather.3.cloned.1.call-done, f32[1536,6144]{1,0:T(8,128)} %param.4), kind=kOutput, calls=%fused_computation.9 | convolution fusion | flops 57982058496 | bytes 53477376 | tf_op jit(solution)/shard_map/dot_general | solution.py:20
  107.4 0.0 copy-start.1
  107.4 0.0 reduce-scatter.3.cloned.1.call-update
  107.4 0.0 all-gather.5.cloned.1.call-start
  107.5 207.4 %reduce-scatter.3.cloned.1.call-done = f32[64,6144]{1,0:T(8,128)} async-done(((f32[512,6144]{1,0:T(8,128)}), f32[64,6144]{1,0:T(8,128)}) %reduce-scatter.3.cloned.1.call-update) | async-done | bytes 1572880 | tf_op jit(solution)/shard_map/reduce_scatter | solution.py:23
  314.9 0.0 copy-done.1
  314.9 3.5 fusion.5
  318.4 0.0 all-gather.5.cloned.1.call-update
  318.4 0.2 reduce-scatter.5.cloned.1.call-start
  318.7 175.5 %all-gather.5.cloned.1.call-done = f32[512,6144]{1,0:T(8,128)} async-done(((f32[64,6144]{1,0:T(8,128)}), f32[512,6144]{1,0:T(8,128)}) %all-gather.5.cloned.1.call-update) | async-done | bytes 12582928 | tf_op jit(solution)/shard_map/all_gather | solution.py:24
  494.1 66.3 %fusion.7 = f32[512,1536]{1,0:T(8,128)} fusion(f32[512,6144]{1,0:T(8,128)} %all-gather.5.cloned.1.call-done, f32[1536,6144]{1,0:T(8,128)} %param.4), kind=kOutput, calls=%fused_computation.10 | convolution fusion | flops 57982058496 | bytes 53477376 | tf_op jit(solution)/shard_map/dot_general | solution.py:33
  560.4 0.0 copy-start
  560.4 0.0 reduce-scatter.5.cloned.1.call-update
  560.4 1.9 copy-done
  562.3 64.5 %convolution_bitcast_fusion = f32[1536,6144]{0,1:T(8,128)} fusion(f32[512,6144]{1,0:T(8,128)} %all-gather.5.cloned.1.call-done, f32[512,1536]{1,0:T(8,128)S(1)} %copy-done), kind=kOutput, calls=%fused_computation | convolution fusion | flops 57982058496 | bytes 53477376 | tf_op jit(solution)/shard_map/dot_general | solution.py:25
  626.8 36.8 %copy.5 = f32[1536,6144]{1,0:T(8,128)} copy(f32[1536,6144]{0,1:T(8,128)} %convolution_bitcast_fusion) | data formatting | bytes 75497472
  663.6 0.0 reduce-scatter.5.cloned.1.call-done
Async XLA Ops:
  7.2 33.7 %all-gather.3.cloned.1.call-start = ((), (), s32[]{:S(2)}) async-start(), calls=%async_computation.2 | async-start | bytes 3932160 | tf_op jit(solution)/shard_map/all_gather | solution.py:19
  7.9 307.0 %reduce-scatter.3.cloned.1.call-start = ((), (), s32[]{:S(2)}) async-start(), calls=%async_computation.3 | async-start | bytes 14155776 | tf_op jit(solution)/shard_map/reduce_scatter | solution.py:23
  107.4 207.5 %copy-start.1 = (f32[64,6144]{1,0:T(8,128)S(1)}, f32[64,6144]{1,0:T(8,128)}, u32[]{:S(2)}) copy-start(f32[64,6144]{1,0:T(8,128)} %param.5) | copy-start | bytes 4718596
  107.4 386.7 %all-gather.5.cloned.1.call-start = ((), (), s32[]{:S(2)}) async-start(), calls=%async_computation.4 | async-start | bytes 14155776 | tf_op jit(solution)/shard_map/all_gather | solution.py:24
  318.4 345.2 %reduce-scatter.5.cloned.1.call-start = ((), (), s32[]{:S(2)}) async-start(), calls=%async_computation.5 | async-start | bytes 3932160 | tf_op jit(solution)/shard_map/reduce_scatter | solution.py:32
  560.4 1.9 copy-start
Sparse Core Ops, SparseCore 0:
  9.6 31.2 all-gather.2
  107.5 207.3 reduce-scatter.2
  318.6 175.5 all-gather.4
  560.5 36.1 reduce-scatter.4
where the time goes:
time: 671 us; the launch traced here: 670 us
  waiting for transfers between devices  416 us (62%)
  matrix products  197 us (29%)
  local copies, waits for them, and re-layouts  38.6 us (6%)
  between operations  13.8 us (2%)
    reduce_scatter x1, waiting for transfers between devices, body(): lax.psum_scatter(partial_pre, 'row', scatter_dimension=0, tiled=True)  207 us
    all_gather x1, waiting for transfers between devices, body(): lax.all_gather(upstream * gelu_slope(shares), 'row', axis=0, tiled=True)  175 us
    dot_general x1, matrix products, body(): jnp.dot(gathered, weights, precision=lax.Precision.HIGHEST, preferred_ele...  66.6 us
    dot_general x1, matrix products, body(): lax.dot_general(delta_pre, weights, (((1,), (1,)), ((), ())), precision=l...  66.3 us
    dot_general x1, matrix products, body(): lax.dot_general(gathered, delta_pre, (((0,), (0,)), ((), ())), precision=...  64.5 us
    unnamed x5, local copies, waits for them, and re-layouts  38.6 us
    all_gather x1, waiting for transfers between devices, body(): gathered = lax.all_gather(activations, 'col', axis=0, tiled=True)  32.9 us
  transfers between devices with their start and end apart: 4, of which 3 were waited for; matrix products, arithmetic and copies ran while one was open for 15% of the time, Pallas kernels for 0%

commit v1 on v0

v1 whole, which is shorter than its diff:
```python
import functools

import jax
import jax.numpy as jnp
from jax import lax
from jax.experimental import pallas as pl
from jax.experimental.pallas import tpu as pltpu
from jax.sharding import PartitionSpec as P

slope_scale = 0.7978845608028654
cubic_term = 0.044715
MESH = pl.DeviceIdType.MESH
LANES = 128
OUTER = 4


def gelu_slope(preact):
    inner = slope_scale * (preact + cubic_term * preact * preact * preact)
    tangent = jnp.tanh(inner)
    return 0.5 * (1.0 + tangent) + 0.5 * preact * (1.0 - tangent * tangent) * slope_scale * (
        1.0 + 3.0 * cubic_term * preact * preact
    )


def split(value):
    high = value.astype(jnp.bfloat16)
    return high, (value - high.astype(jnp.float32)).astype(jnp.bfloat16)


def dot3(a_high, a_low, b_high, b_low, dims):
    def one(a, b):
        return lax.dot_general(a, b, (dims, ((), ())), preferred_element_type=jnp.float32)

    return one(a_high, b_high) + (one(a_high, b_low) + one(a_low, b_high))


class Stream:
    def __init__(self, first, second, refs, tokens):
        self.axes = (first, second)
        self.state, self.land_first, self.land_second, self.send, self.recv, self.ready = refs
        (n_f, _, _), (n_g, _, _) = first, second
        self.big, self.small = tokens // n_f, tokens // (n_f * n_g)
        self.hops = (
            [("sum", 0, h) for h in range(1, n_f)]
            + [("sum", 1, h) for h in range(1, n_g)]
            + [("spread", 1, h) for h in range(1, n_g)]
            + [("spread", 0, h) for h in range(1, n_f)]
        )
        self.sums = n_f + n_g - 2

    def region(self, axis, block):
        if axis == 0:
            return pl.ds(pl.multiple_of(block * self.big, self.big), self.big)
        mine = self.axes[0][1] * self.big
        return pl.ds(pl.multiple_of(mine + block * self.small, self.small), self.small)

    def own(self):
        return self.region(1, self.axes[1][1])

    def copy(self, j, way, slot, block, row, col):
        kind, axis, h = self.hops[j]
        n, me, stride = self.axes[axis]
        peer = row + stride if way == 0 else row - stride
        source = self.state.at[slot, self.region(axis, block)]
        if kind == "sum":
            land = self.land_first if axis == 0 else self.land_second
            target = land.at[h - 1, way]
        else:
            target = source
        return pltpu.make_async_remote_copy(
            src_ref=source,
            dst_ref=target,
            send_sem=self.send.at[j, way],
            recv_sem=self.recv.at[j, way],
            device_id=(peer, col),
            device_id_type=MESH,
        )

    def sending(self, j, way):
        kind, axis, h = self.hops[j]
        n, me, _ = self.axes[axis]
        if kind == "sum":
            if way == 0:
                return jnp.logical_and(me <= h - 1, me < n - 1), n - h + me
            return jnp.logical_and(n - 1 - me <= h - 1, me > 0), h - n + me
        if way == 0:
            return jnp.logical_and(me >= h - 1, me < n - 1), me - (h - 1)
        return jnp.logical_and(n - 1 - me >= h - 1, me > 0), me + (h - 1)

    def receiving(self, j, way):
        kind, axis, h = self.hops[j]
        n, me, _ = self.axes[axis]
        if kind == "sum":
            if way == 0:
                return jnp.logical_and(me <= h, me >= 1), n - h + me - 1
            return jnp.logical_and(n - 1 - me <= h, me <= n - 2), h - n + me + 1
        if way == 0:
            return me >= h, me - h
        return n - 1 - me >= h, me + h

    def issue(self, step, chunks, slots, row, col):
        for j in range(len(self.hops)):
            chunk = step - 1 - j
            valid = jnp.logical_and(chunk >= 0, chunk < chunks)
            slot = lax.rem(chunk + slots, slots)
            for way in range(2):
                on, block = self.sending(j, way)

                @pl.when(jnp.logical_and(valid, on))
                def _(j=j, way=way, slot=slot, block=block):
                    self.copy(j, way, slot, block, row, col).start()

    def settle(self, step, chunks, slots, row, col, finish):
        for j in range(len(self.hops)):
            chunk = step - 2 - j
            valid = jnp.logical_and(chunk >= 0, chunk < chunks)
            slot = lax.rem(chunk + 2 * slots, slots)
            kind, axis, h = self.hops[j]
            for way in range(2):
                sent, out_block = self.sending(j, way)

                @pl.when(jnp.logical_and(valid, sent))
                def _(j=j, way=way, slot=slot, block=out_block):
                    self.copy(j, way, slot, block, row, col).wait_send()

                got, in_block = self.receiving(j, way)

                @pl.when(jnp.logical_and(valid, got))
                def _(j=j, way=way, slot=slot, block=in_block, kind=kind, axis=axis, h=h):
                    self.copy(j, way, slot, block, row, col).wait_recv()
                    if kind == "sum":
                        land = self.land_first if axis == 0 else self.land_second
                        here = self.region(axis, block)
                        self.state[slot, here, :] = self.state[slot, here, :] + land[h - 1, way]

            if j == self.sums - 1:

                @pl.when(valid)
                def _(slot=slot, chunk=chunk):
                    finish(slot, chunk)


def exchange_kernel(
    outer,
    inner,
    act_ref,
    up_ref,
    w_ref,
    high_ref,
    low_ref,
    grad_ref,
    w_in,
    w_high,
    w_low,
    g_high,
    g_low,
    state_a,
    state_b,
    land_a1,
    land_a2,
    land_b1,
    land_b2,
    send_a,
    recv_a,
    send_b,
    recv_b,
    ready_a,
    ready_b,
    w_sem,
):
    tokens, depth = act_ref.shape
    columns = up_ref.shape[1]
    width = 2 * LANES
    chunks = columns // width
    slots = state_a.shape[0]
    part = tokens // (outer * inner)
    tile = min(256, tokens)
    row, col = lax.axis_index("row"), lax.axis_index("col")
    at_outer, at_inner = row // inner, lax.rem(row, inner)
    along_outer = (outer, at_outer, inner)
    along_inner = (inner, at_inner, 1)
    stream_a = Stream(along_inner, along_outer, (state_a, land_a1, land_a2, send_a, recv_a, ready_a), tokens)
    stream_b = Stream(along_outer, along_inner, (state_b, land_b1, land_b2, send_b, recv_b, ready_b), tokens)

    neighbours = []
    for index, (n, me, stride) in enumerate((along_inner, along_outer)):
        neighbours.append((me < n - 1, row + stride, 2 * index, 2 * index + 1))
        neighbours.append((me > 0, row - stride, 2 * index + 1, 2 * index))

    barrier = pltpu.get_barrier_semaphore()
    for there, peer, _, _ in neighbours:

        @pl.when(there)
        def _(peer=peer):
            pl.semaphore_signal(barrier, inc=1, device_id=(peer, col), device_id_type=MESH)

    pl.semaphore_wait(barrier, sum(there.astype(jnp.int32) for there, _, _, _ in neighbours))

    def meet(ready):
        for there, peer, _, theirs in neighbours:

            @pl.when(there)
            def _(peer=peer, theirs=theirs):
                pl.semaphore_signal(ready.at[theirs], inc=1, device_id=(peer, col), device_id_type=MESH)

        for there, _, mine, _ in neighbours:

            @pl.when(there)
            def _(mine=mine):
                pl.semaphore_wait(ready.at[mine], 1)

    def load(chunk):
        at = pl.ds(pl.multiple_of(chunk * width, width), width)
        here = lax.rem(chunk, 2)
        return pltpu.make_async_copy(w_ref.at[:, at], w_in.at[here], w_sem.at[here])

    load(0).start()

    @pl.loop(0, tokens // tile)
    def _(i):
        at = pl.ds(pl.multiple_of(i * tile, tile), tile)
        g_high[at, :], g_low[at, :] = split(act_ref[at, :])

    grad_ref[...] = jnp.zeros_like(grad_ref)

    def finish(stream, half):
        def run(slot, chunk):
            own = stream.own()
            at = pl.ds(pl.multiple_of(chunk * width + half * LANES, LANES), LANES)
            stream.state[slot, own, :] = up_ref[:, at] * gelu_slope(stream.state[slot, own, :])

        return run

    def swapped(index):
        place = lax.rem(index, inner) * outer + index // inner
        return pl.ds(pl.multiple_of(place * part, part), part)

    w_tile = 128

    def forward(chunk):
        slot = lax.rem(chunk, slots)
        here = lax.rem(chunk, 2)

        @pl.loop(0, depth // w_tile)
        def _(i):
            at = pl.ds(pl.multiple_of(i * w_tile, w_tile), w_tile)
            w_high[slot, at, :], w_low[slot, at, :] = split(w_in[here, at, :])

        @pl.loop(0, tokens // tile)
        def _(i):
            at = pl.ds(pl.multiple_of(i * tile, tile), tile)
            product = dot3(
                g_high[at, :], g_low[at, :], w_high[slot], w_low[slot], ((1,), (0,))
            )
            state_b[slot, at, :] = product[:, LANES:]
            for q in range(tile // part):
                state_a[slot, swapped(i * (tile // part) + q), :] = product[
                    q * part : (q + 1) * part, :LANES
                ]

    def backward(chunk):
        slot = lax.rem(chunk, slots)
        left = pl.ds(pl.multiple_of(chunk * width, width), LANES)
        right = pl.ds(pl.multiple_of(chunk * width + LANES, LANES), LANES)
        both = pl.ds(pl.multiple_of(chunk * width, width), width)

        @pl.loop(0, tokens // part)
        def _(i):
            at = pl.ds(pl.multiple_of(i * part, part), part)
            high_ref[at, left], low_ref[at, left] = split(state_a[slot, swapped(i), :])
            high_ref[at, right], low_ref[at, right] = split(state_b[slot, at, :])

        @pl.loop(0, tokens // tile)
        def _(i):
            at = pl.ds(pl.multiple_of(i * tile, tile), tile)
            grad_ref[at, :] += dot3(
                high_ref[at, both], low_ref[at, both], w_high[slot], w_low[slot], ((1,), (1,))
            )

    hops = len(stream_a.hops)

    @pl.loop(0, chunks + hops + 1)
    def _(step):
        stream_a.settle(step, chunks, slots, row, col, finish(stream_a, 0))
        meet(ready_a)
        stream_a.issue(step, chunks, slots, row, col)

        @pl.when(step < chunks)
        def _():
            load(step).wait()

            @pl.when(step + 1 < chunks)
            def _():
                load(step + 1).start()

            forward(step)

        stream_b.settle(step, chunks, slots, row, col, finish(stream_b, 1))
        meet(ready_b)
        stream_b.issue(step, chunks, slots, row, col)

        @pl.when(step >= hops + 1)
        def _():
            backward(step - (hops + 1))


def exchange(activations, upstream, weights, outer, inner):
    tokens, depth = activations.shape
    columns = weights.shape[1]
    width = 2 * LANES
    hops = 2 * (outer + inner - 2)
    slots = hops + 2
    f32, bf16 = jnp.float32, jnp.bfloat16
    small = tokens // (outer * inner)
    whole = pl.BlockSpec(memory_space=pltpu.VMEM)
    return pl.pallas_call(
        functools.partial(exchange_kernel, outer, inner),
        out_shape=(
            jax.ShapeDtypeStruct((tokens, columns), bf16),
            jax.ShapeDtypeStruct((tokens, columns), bf16),
            jax.ShapeDtypeStruct((tokens, depth), f32),
        ),
        in_specs=[whole, whole, pl.BlockSpec(memory_space=pl.ANY)],
        out_specs=(whole, whole, whole),
        scratch_shapes=[
            pltpu.VMEM((2, depth, width), f32),
            pltpu.VMEM((slots, depth, width), bf16),
            pltpu.VMEM((slots, depth, width), bf16),
            pltpu.VMEM((tokens, depth), bf16),
            pltpu.VMEM((tokens, depth), bf16),
            pltpu.VMEM((slots, tokens, LANES), f32),
            pltpu.VMEM((slots, tokens, LANES), f32),
            pltpu.VMEM((inner - 1, 2, tokens // inner, LANES), f32),
            pltpu.VMEM((outer - 1, 2, small, LANES), f32),
            pltpu.VMEM((outer - 1, 2, tokens // outer, LANES), f32),
            pltpu.VMEM((inner - 1, 2, small, LANES), f32),
            pltpu.SemaphoreType.DMA((hops, 2)),
            pltpu.SemaphoreType.DMA((hops, 2)),
            pltpu.SemaphoreType.DMA((hops, 2)),
            pltpu.SemaphoreType.DMA((hops, 2)),
            pltpu.SemaphoreType.REGULAR((4,)),
            pltpu.SemaphoreType.REGULAR((4,)),
            pltpu.SemaphoreType.DMA((2,)),
        ],
        compiler_params=pltpu.CompilerParams(
            collective_id=0, has_side_effects=True, vmem_limit_bytes=58 * 1024 * 1024
        ),
        cost_estimate=pl.CostEstimate(
            flops=12 * tokens * depth * columns,
            bytes_accessed=4 * depth * columns,
            transcendentals=small * columns,
        ),
    )(activations, upstream, weights)


def outer_product_kernel(act_ref, high_ref, low_ref, out_ref, a_high, a_low):
    @pl.when(pl.program_id(0) == 0)
    def _():
        a_high[...], a_low[...] = split(act_ref[...])

    tile = 256 if out_ref.shape[0] % 256 == 0 else 128

    @pl.loop(0, out_ref.shape[0] // tile)
    def _(i):
        at = pl.ds(pl.multiple_of(i * tile, tile), tile)
        out_ref[at, :] = dot3(
            a_high[at, :], a_low[at, :], high_ref[...], low_ref[...], ((1,), (0,))
        )


def outer_product(features, high, low):
    depth, tokens = features.shape
    columns = high.shape[1]
    width = 512
    return pl.pallas_call(
        outer_product_kernel,
        out_shape=jax.ShapeDtypeStruct((depth, columns), jnp.float32),
        grid=(columns // width,),
        in_specs=[
            pl.BlockSpec((depth, tokens), lambda i: (0, 0)),
            pl.BlockSpec((tokens, width), lambda i: (0, i)),
            pl.BlockSpec((tokens, width), lambda i: (0, i)),
        ],
        out_specs=pl.BlockSpec((depth, width), lambda i: (0, i)),
        scratch_shapes=[
            pltpu.VMEM((depth, tokens), jnp.bfloat16),
            pltpu.VMEM((depth, tokens), jnp.bfloat16),
        ],
        compiler_params=pltpu.CompilerParams(vmem_limit_bytes=40 * 1024 * 1024),
        cost_estimate=pl.CostEstimate(
            flops=6 * tokens * depth * columns,
            bytes_accessed=4 * depth * columns + 4 * tokens * columns,
            transcendentals=0,
        ),
    )(features, high, low)


def body(rows, activations, weights, upstream):
    gathered = lax.all_gather(activations, "col", axis=0, tiled=True)
    high, low, grad = exchange(gathered, upstream, weights, OUTER, rows // OUTER)
    input_grad = lax.psum_scatter(grad, "col", scatter_dimension=0, tiled=True)
    weight_grad = outer_product(gathered.T, high, low)
    return (input_grad, weight_grad)


def solution(mesh):
    placed = (P("col", "row"), P("row", "col"), P("row", "col"))
    return jax.shard_map(
        functools.partial(body, mesh.shape["row"]),
        mesh=mesh,
        in_specs=placed,
        out_specs=(P("col", "row"), P("row", "col")),
        check_vma=False,
    )
```

time: 671 us -> 363 us (0.54)
  waiting for transfers between devices: 416 us -> 32.3 us
  Pallas kernels: 0 us -> 308 us
  matrix products: 197 us -> 0 us
  local copies, waits for them, and re-layouts: 38.6 us -> 8.6 us
    pallas_call x0 -> x2, Pallas kernels: none -> 308 us  [the longest x1 263 us: exchange(): pl.pallas_call(functools.partial(exchange_kernel, outer, inner), out_shap...]
    reduce_scatter x2 -> x1, waiting for transfers between devices: 207 us -> 0.01 us  [body(): input_grad = lax.psum_scatter(grad, 'col', scatter_dimension=0, tiled=True)]
    dot_general x3 -> x0, matrix products: 197 us -> none  [the longest x1 66.6 us: body(): jnp.dot(gathered, weights, precision=lax.Precision.HIGHEST, preferred_ele...]
    all_gather x1 -> x0, waiting for transfers between devices: 175 us -> none  [body(): lax.all_gather(upstream * gelu_slope(shares), 'row', axis=0, tiled=True)]
    unnamed x5, local copies, waits for them, and re-layouts: 38.6 us -> 5.06 us
  transfers between devices with their start and end apart: 4 -> 2, of which waited for: 3 -> 1; matrix products, arithmetic and copies ran while one was open for 15% -> 0% of each run, Pallas kernels for 0% -> 12%
where the time goes in v1:
time: 363 us
  Pallas kernels  308 us (85%)
  waiting for transfers between devices  32.3 us (9%)
  between operations  14.1 us (4%)
  local copies, waits for them, and re-layouts  8.6 us (2%)
    pallas_call x1, Pallas kernels, exchange(): pl.pallas_call(functools.partial(exchange_kernel, outer, inner), out_shap...  263 us
    pallas_call x1, Pallas kernels, outer_product(): pl.pallas_call(outer_product_kernel, out_shape=jax.ShapeDtypeStruct((dept...  44.9 us
    all_gather x1, waiting for transfers between devices, body(): gathered = lax.all_gather(activations, 'col', axis=0, tiled=True)  32.2 us
  transfers between devices with their start and end apart: 2, of which 1 were waited for; matrix products, arithmetic and copies ran while one was open for 0% of the time, Pallas kernels for 12%

profile of v1, /device:TPU:0, one launch (start us, length us, event | category | flops | bytes accessed | tf_op | source)
XLA Modules:
  0.0 362.7 jit_solution(11072384520956520810)
XLA Ops:
  7.2 0.0 all-gather.2.cloned.1.call-start
  7.2 2.3 copy.5
  9.5 0.0 all-gather.2.cloned.1.call-update
  9.5 0.0 reduce-scatter.2.cloned.1.call-start
  9.6 32.2 %all-gather.2.cloned.1.call-done = f32[512,1536]{0,1:T(8,128)} async-done(((f32[128,1536]{0,1:T(8,128)}), f32[512,1536]{0,1:T(8,128)}) %all-gather.2.cloned.1.call-update) | async-done | bytes 3145744 | tf_op jit(solution)/shard_map/all_gather | solution.py:399
  41.8 3.5 copy.6.act_ref
  45.3 0.0 copy-start
  45.3 262.7 %shard_map.50 = (bf16[512,6144]{1,0:T(8,128)(2,1)}, bf16[512,6144]{1,0:T(8,128)(2,1)}, f32[512,1536]{1,0:T(8,128)}) custom-call(f32[512,1536]{1,0:T(8,128)} %copy.6.act_ref, f32[64,6144]{1,0:T(8,128)} %up_ref.1, f32[1536,6144]{1,0:T(8,128)} %w_ref.1), custom_call_target="tpu_custom_call" | custom-call | flops 57982058496 | bytes 37748736 | tf_op jit(solution)/shard_map/pallas_call | solution.py:316
  308.1 0.0 reduce-scatter.2.cloned.1.call-update
  308.1 0.0 copy-done
  308.1 0.0 copy-start.1
  308.1 2.8 copy-done.1
  310.9 44.9 %shard_map.51 = f32[1536,6144]{1,0:T(8,128)} custom-call(f32[1536,512]{1,0:T(8,128)S(1)} %bitcast.1, bf16[512,6144]{1,0:T(8,128)(2,1)S(1)} %copy-done.1, bf16[512,6144]{1,0:T(8,128)(2,1)} %get-tuple-element.7.low_ref), custom_call_target="tpu_custom_call" | custom-call | flops 28991029248 | bytes 50331648 | tf_op jit(solution)/shard_map/pallas_call | solution.py:375
  355.8 0.0 reduce-scatter.2.cloned.1.call-done
Async XLA Ops:
  7.2 34.6 %all-gather.2.cloned.1.call-start = ((), (), s32[]{:S(2)}) async-start(), calls=%async_computation.1 | async-start | bytes 3932160 | tf_op jit(solution)/shard_map/all_gather | solution.py:399
  9.5 346.3 %reduce-scatter.2.cloned.1.call-start = ((), (), s32[]{:S(2)}) async-start(), calls=%async_computation.2 | async-start | bytes 3932160 | tf_op jit(solution)/shard_map/reduce_scatter | solution.py:401
  45.3 262.8 %copy-start = (f32[512,1536]{0,1:T(8,128)S(1)}, f32[512,1536]{0,1:T(8,128)}, u32[]{:S(2)}) copy-start(f32[512,1536]{0,1:T(8,128)} %all-gather.2.cloned.1.call-done) | copy-start | bytes 9437188
  308.1 2.8 copy-start.1
Sparse Core Ops, SparseCore 0:
  10.1 31.6 all-gather.1
  308.2 36.4 reduce-scatter.1

commit v2 on v1

--- a/solution.py
+++ b/solution.py
@@ -353,23 +353,29 @@
     )(activations, upstream, weights)
 
 
-def outer_product_kernel(act_ref, high_ref, low_ref, out_ref, a_high, a_low):
+def outer_product_kernel(act_ref, high_ref, low_ref, out_ref, left, right):
+    tokens = act_ref.shape[0]
+
     @pl.when(pl.program_id(0) == 0)
     def _():
-        a_high[...], a_low[...] = split(act_ref[...])
-
+        high, low = split(act_ref[...].T)
+        left[:, :tokens] = high
+        left[:, tokens : 2 * tokens] = high
+        left[:, 2 * tokens :] = low
+
+    right[:tokens, :] = high_ref[...]
+    right[tokens : 2 * tokens, :] = low_ref[...]
+    right[2 * tokens :, :] = high_ref[...]
     tile = 256 if out_ref.shape[0] % 256 == 0 else 128
 
     @pl.loop(0, out_ref.shape[0] // tile)
     def _(i):
         at = pl.ds(pl.multiple_of(i * tile, tile), tile)
-        out_ref[at, :] = dot3(
-            a_high[at, :], a_low[at, :], high_ref[...], low_ref[...], ((1,), (0,))
-        )
+        out_ref[at, :] = jnp.dot(left[at, :], right[...], preferred_element_type=jnp.float32)
 
 
 def outer_product(features, high, low):
-    depth, tokens = features.shape
+    tokens, depth = features.shape
     columns = high.shape[1]
     width = 512
     return pl.pallas_call(
@@ -377,14 +383,14 @@
         out_shape=jax.ShapeDtypeStruct((depth, columns), jnp.float32),
         grid=(columns // width,),
         in_specs=[
-            pl.BlockSpec((depth, tokens), lambda i: (0, 0)),
+            pl.BlockSpec((tokens, depth), lambda i: (0, 0)),
             pl.BlockSpec((tokens, width), lambda i: (0, i)),
             pl.BlockSpec((tokens, width), lambda i: (0, i)),
         ],
         out_specs=pl.BlockSpec((depth, width), lambda i: (0, i)),
         scratch_shapes=[
-            pltpu.VMEM((depth, tokens), jnp.bfloat16),
-            pltpu.VMEM((depth, tokens), jnp.bfloat16),
+            pltpu.VMEM((depth, 3 * tokens), jnp.bfloat16),
+            pltpu.VMEM((3 * tokens, width), jnp.bfloat16),
         ],
         compiler_params=pltpu.CompilerParams(vmem_limit_bytes=40 * 1024 * 1024),
         cost_estimate=pl.CostEstimate(
@@ -399,7 +405,7 @@
     gathered = lax.all_gather(activations, "col", axis=0, tiled=True)
     high, low, grad = exchange(gathered, upstream, weights, OUTER, rows // OUTER)
     input_grad = lax.psum_scatter(grad, "col", scatter_dimension=0, tiled=True)
-    weight_grad = outer_product(gathered.T, high, low)
+    weight_grad = outer_product(gathered, high, low)
     return (input_grad, weight_grad)
 
 

time: 363 us -> 360 us (level)
  local copies, waits for them, and re-layouts: 8.6 us -> 2.78 us
  transfers between devices with their start and end apart: 2 -> 2, of which waited for: 1 -> 1; matrix products, arithmetic and copies ran while one was open for 0% -> 0% of each run, Pallas kernels for 12% -> 13%
where the time goes in v2:
time: 360 us
  Pallas kernels  310 us (86%)
  waiting for transfers between devices  33.6 us (9%)
  between operations  14.1 us (4%)
    pallas_call x1, Pallas kernels, exchange(): pl.pallas_call(functools.partial(exchange_kernel, outer, inner), out_shap...  263 us
    pallas_call x1, Pallas kernels, outer_product(): pl.pallas_call(outer_product_kernel, out_shape=jax.ShapeDtypeStruct((dept...  46.7 us
    all_gather x1, waiting for transfers between devices, body(): gathered = lax.all_gather(activations, 'col', axis=0, tiled=True)  32.9 us
  transfers between devices with their start and end apart: 2, of which 1 were waited for; matrix products, arithmetic and copies ran while one was open for 0% of the time, Pallas kernels for 13%

profile of v2, /device:TPU:0, one launch (start us, length us, event | category | flops | bytes accessed | tf_op | source)
XLA Modules:
  0.0 360.2 jit_solution(6986790547163777265)
XLA Ops:
  7.2 0.0 all-gather.2.cloned.1.call-start
  7.2 0.7 all-gather.2.cloned.1.call-update
  7.9 0.0 reduce-scatter.2.cloned.1.call-start
  7.9 32.9 %all-gather.2.cloned.1.call-done.act_ref = f32[512,1536]{1,0:T(8,128)} async-done(((f32[128,1536]{1,0:T(8,128)}), f32[512,1536]{1,0:T(8,128)}) %all-gather.2.cloned.1.call-update) | async-done | bytes 3145744 | tf_op jit(solution)/shard_map/all_gather | solution.py:405
  40.8 0.0 copy-start
  40.8 263.1 %shard_map.50 = (bf16[512,6144]{1,0:T(8,128)(2,1)}, bf16[512,6144]{1,0:T(8,128)(2,1)}, f32[512,1536]{1,0:T(8,128)}) custom-call(f32[512,1536]{1,0:T(8,128)} %all-gather.2.cloned.1.call-done.act_ref, f32[64,6144]{1,0:T(8,128)} %up_ref.1, f32[1536,6144]{1,0:T(8,128)} %w_ref.1), custom_call_target="tpu_custom_call" | custom-call | flops 57982058496 | bytes 37748736 | tf_op jit(solution)/shard_map/pallas_call | solution.py:316
  303.9 0.0 reduce-scatter.2.cloned.1.call-update
  303.9 0.0 copy-done
  303.9 0.0 copy-start.1
  303.9 2.8 copy-done.1
  306.7 46.7 %shard_map.51 = f32[1536,6144]{1,0:T(8,128)} custom-call(f32[512,1536]{1,0:T(8,128)S(1)} %copy-done, bf16[512,6144]{1,0:T(8,128)(2,1)S(1)} %copy-done.1, bf16[512,6144]{1,0:T(8,128)(2,1)} %get-tuple-element.7.low_ref), custom_call_target="tpu_custom_call" | custom-call | flops 28991029248 | bytes 50331648 | tf_op jit(solution)/shard_map/pallas_call | solution.py:381
  353.4 0.0 reduce-scatter.2.cloned.1.call-done
Async XLA Ops:
  7.2 33.7 %all-gather.2.cloned.1.call-start = ((), (), s32[]{:S(2)}) async-start(), calls=%async_computation.1 | async-start | bytes 3932160 | tf_op jit(solution)/shard_map/all_gather | solution.py:405
  7.9 345.5 %reduce-scatter.2.cloned.1.call-start = ((), (), s32[]{:S(2)}) async-start(), calls=%async_computation.2 | async-start | bytes 3932160 | tf_op jit(solution)/shard_map/reduce_scatter | solution.py:407
  40.8 263.1 %copy-start = (f32[512,1536]{1,0:T(8,128)S(1)}, f32[512,1536]{1,0:T(8,128)}, u32[]{:S(2)}) copy-start(f32[512,1536]{1,0:T(8,128)} %all-gather.2.cloned.1.call-done.act_ref) | copy-start | bytes 9437188
  303.9 2.8 copy-start.1
Sparse Core Ops, SparseCore 0:
  9.6 31.2 all-gather.1
  304.0 36.0 reduce-scatter.1
